TPU v7x, 512 devices: a whole 4x8x8 slice. The times are simulated.
512 devices in a mesh: rep: 64 (over x, z_hi, y), tp: 8 (over z_lo, core).
Axes of the slice: x: 4, y: 8, z: 8 (z_hi: 2, z_lo: 4; z = z_hi * 4 + z_lo), core: 2. Of those that a mesh axis runs over, the one named last changes fastest.
Arguments:
- weight: bfloat16 [64, 2048, 2048], P('rep', None, 'tp'), may hold values from -6 to 6
- second_moment: bfloat16 [64, 2048, 2048], P('rep', None, 'tp'), may hold values from 0.0009994507 to 1
- inputs: bfloat16 [2, 64, 1024, 2048], P(None, 'rep', 'tp'), may hold values from -6 to 6
- cotangent: bfloat16 [2, 64, 1024, 2048], P(None, 'rep', None, 'tp'), may hold values from -6 to 6
- gossip_steps: int32 [2], replicated, may hold values from 0 to 5, as said below
Outputs:
- averaged: bfloat16 [64, 2048, 2048], P('rep', None, 'tp')
Inputs may be any that keep to these rules, and one draw needn't show every extreme that they name: `gossip_steps`: the two entries differ; one of them is 5.
All inputs are finite; a program needn't handle non-finite values.
Results may differ from a plain program's by a relative error of at most 0.015.
Values may be sent and summed in bfloat16 or wider, within the bound.
A program may use at most 64 MiB of HBM per device.

v0:
```python
from functools import partial
import math

import jax
import jax.numpy as jnp
from jax import lax
from jax.sharding import PartitionSpec as P


def shortened(value):
    return jax.tree.map(lambda a: a.astype(jnp.bfloat16) if a.dtype == jnp.float32 else a, value)


def partner(block, axis, apart):
    count = lax.axis_size(axis)
    route = []
    for low in range(count):
        high = low | 1 << apart
        if high != low and high < count:
            route += [(low, high), (high, low)]
    return lax.ppermute(block, axis, route)


def adam_update(weight, first, second, grad):
    first_new = 0.9 * first.astype(jnp.float32) + 0.1 * grad
    second_new = 0.95 * second.astype(jnp.float32) + 0.05 * grad * grad
    moved = weight.astype(jnp.float32) - 0.2 * first_new / (jnp.sqrt(second_new) + 1e-08)
    return (
        moved.astype(jnp.bfloat16),
        first_new.astype(jnp.bfloat16),
        second_new.astype(jnp.bfloat16),
    )


def swap_with(bit, tensor):
    return jax.tree.map(
        lambda part, own: part.astype(own.dtype), partner(shortened(tensor), "rep", bit), tensor
    )


def per_device(weight, second_moment, inputs, cotangent, gossip_steps):
    tensor = weight[0]
    first = jnp.zeros_like(tensor)
    second = second_moment[0]
    factor = 1.0 / math.sqrt(inputs.shape[3])
    bits = lax.axis_size("rep").bit_length() - 1
    branches = [partial(swap_with, bit) for bit in range(bits)]
    for step in range(2):
        back = cotangent[step, 0]
        grad = jnp.einsum(
            "rk,rn->kn",
            lax.all_gather(inputs[step, 0], "tp", axis=0, tiled=True),
            back,
            preferred_element_type=jnp.float32,
        )
        tensor, first, second = adam_update(tensor, first, second, grad * factor)
        other = lax.switch(gossip_steps[step], branches, tensor)
        tensor = ((tensor.astype(jnp.float32) + other.astype(jnp.float32)) * 0.5).astype(
            jnp.bfloat16
        )
    return tensor[None]


def solution(mesh):
    in_specs = (
        P("rep", None, "tp"),
        P("rep", None, "tp"),
        P(None, "rep", "tp", None),
        P(None, "rep", None, "tp"),
        P(),
    )
    out_specs = P("rep", None, "tp")
    return jax.shard_map(
        per_device, mesh=mesh, in_specs=in_specs, out_specs=out_specs, check_vma=False
    )
```

profile of v0, /device:TPU:2, one launch (start us, length us, event | category | flops | bytes accessed | tf_op | source)
XLA Modules:
  0.0 172.7 jit_solution(9495070244193242996)
XLA Ops:
  6.5 0.0 copy-start
  6.5 0.0 copy-start.3
  6.5 0.0 copy-start.2
  6.5 0.0 copy-start.1
  6.5 0.0 all-gather.5.cloned.1.call-start
  6.6 2.5 %fusion.12 = (bf16[1,1,128,2048]{3,2,1,0:T(8,128)(2,1)}, bf16[1,1,128,2048]{3,2,1,0:T(8,128)(2,1)}) fusion(bf16[2,1,128,2048]{3,2,1,0:T(8,128)(2,1)} %param.19), kind=kLoop, calls=%fused_computation.16 | loop fusion | bytes 2097152 | tf_op jit(solution)/shard_map/slice | solution.py:52
  9.0 0.0 all-gather.5.cloned.1.call-update
  9.1 0.0 all-gather.7.cloned.1.call-start
  9.1 0.7 all-gather.7.cloned.1.call-update
  9.8 0.0 copy-done
  9.8 0.6 fusion.13
  11.8 60.1 %all-gather.5.cloned.1.call-done = bf16[1,1,1024,2048]{3,2,1,0:T(8,128)(2,1)} async-done(((bf16[1,1,128,2048]{3,2,1,0:T(8,128)(2,1)}), bf16[1,1,1024,2048]{3,2,1,0:T(8,128)(2,1)}) %all-gather.5.cloned.1.call-update) | async-done | bytes 4194320 | tf_op jit(solution)/shard_map/all_gather | solution.py:52
  71.9 0.0 copy-done.3
  71.9 0.0 copy-done.2
  71.9 0.0 copy-done.1
  71.9 5.9 %fusion.4 = (bf16[2048,256]{1,0:T(8,128)(2,1)S(1)}, f32[2048,256]{1,0:T(8,128)}) fusion(bf16[1,2048,256]{2,1,0:T(8,128)(2,1)S(1)} %copy-done.1, bf16[1,2048,256]{2,1,0:T(8,128)(2,1)S(1)} %copy-done.2, bf16[2,1,1024,256]{3,2,1,0:T(8,128)(2,1)S(1)} %copy-done.3, bf16[1,1,1024,2048]{3,2,1,0:T(8,128)(2,1)} %all-gather.5.cloned.1.call-done), kind=kOutput, calls=%fused_computation.5 | convolution fusion | flops 1080033280 | bytes 9961472 | tf_op jit(solution)/shard_map/rk,rn->kn/dot_general | solution.py:50
  77.8 47.5 %conditional.8 = (bf16[2048,256]{1,0:T(8,128)(2,1)}) conditional(s32[]{:T(128)} %bitcast.4, bf16[2048,256]{1,0:T(8,128)(2,1)S(1)} %get-tuple-element.47, bf16[2048,256]{1,0:T(8,128)(2,1)S(1)} %get-tuple-element.47, bf16[2048,256]{1,0:T(8,128)(2,1)S(1)} %get-tuple-element.47, ...), branch_computations={%region_0.0_spmd, %region_1.0_spmd, %region_2.0_spmd, %region_3.0_... | conditional | bytes 4194352
  77.8 4.3 %collective-permute-start.1 = (bf16[2048,256]{1,0:T(8,128)(2,1)S(1)}, bf16[2048,256]{1,0:T(8,128)(2,1)}, u32[]{:S(2)}, u32[]{:S(2)}) collective-permute-start(bf16[2048,256]{1,0:T(8,128)(2,1)S(1)} %param.1), channel_id=1, source_target_pairs={{0,16},{16,0},{8,24},{24,8},{32,48},{48,32},{40,56},{56,40},{64,80... | collective-permute-start | bytes 3145736 | tf_op jit(solution)/shard_map/cond/branch_1_fun/ppermute | solution.py:21
  82.1 43.2 %collective-permute-done.1 = bf16[2048,256]{1,0:T(8,128)(2,1)} collective-permute-done((bf16[2048,256]{1,0:T(8,128)(2,1)S(1)}, bf16[2048,256]{1,0:T(8,128)(2,1)}, u32[]{:S(2)}, u32[]{:S(2)}) %collective-permute-start.1) | collective-permute-done | bytes 1048608 | tf_op jit(solution)/shard_map/cond/branch_1_fun/ppermute | solution.py:21
  125.3 5.1 %all-gather.7.cloned.1.call-done = bf16[1,1,1024,2048]{3,2,1,0:T(8,128)(2,1)} async-done(((bf16[1,1,128,2048]{3,2,1,0:T(8,128)(2,1)}), bf16[1,1,1024,2048]{3,2,1,0:T(8,128)(2,1)}) %all-gather.7.cloned.1.call-update) | async-done | bytes 4194320 | tf_op jit(solution)/shard_map/all_gather | solution.py:52
  130.4 7.3 %subtract_convert_fusion = bf16[2048,256]{1,0:T(8,128)(2,1)S(1)} fusion(bf16[1,1,1024,2048]{3,2,1,0:T(8,128)(2,1)} %all-gather.7.cloned.1.call-done, bf16[2048,256]{1,0:T(8,128)(2,1)} %get-tuple-element.49, f32[2048,256]{1,0:T(8,128)} %get-tuple-element.48, bf16[1,2048,256]{2,1,0:T(8,128)(2,1)S(1)} %copy-done.2, bf16[2,1,1024,256]{3,2,1,0:T(8,128)(2,1)} %param.20, ...), kind=kOutput, calls=%fused_computation.8 | convolution fusion | flops 1092616192 | bytes 11010048 | tf_op jit(solution)/shard_map/rk,rn->kn/dot_general | solution.py:50
  137.7 25.7 %conditional.9 = (bf16[2048,256]{1,0:T(8,128)(2,1)}) conditional(s32[]{:T(128)} %bitcast.7, bf16[2048,256]{1,0:T(8,128)(2,1)S(1)} %subtract_convert_fusion, bf16[2048,256]{1,0:T(8,128)(2,1)S(1)} %subtract_convert_fusion, bf16[2048,256]{1,0:T(8,128)(2,1)S(1)} %subtract_convert_fusion, ...), branch_computations={%region_6.0_spmd, %region_7.0_spmd, %region_8.0_spmd, %region_9.0_... | conditional | bytes 4194352
  137.7 4.0 %collective-permute-start.11 = (bf16[2048,256]{1,0:T(8,128)(2,1)S(1)}, bf16[2048,256]{1,0:T(8,128)(2,1)}, u32[]{:S(2)}, u32[]{:S(2)}) collective-permute-start(bf16[2048,256]{1,0:T(8,128)(2,1)S(1)} %param.11), channel_id=1, source_target_pairs={{0,256},{256,0},{8,264},{264,8},{16,272},{272,16},{24,280},{280,24... | collective-permute-start | bytes 3145736 | tf_op jit(solution)/shard_map/cond/branch_5_fun/ppermute | solution.py:21
  141.7 21.7 %collective-permute-done.11 = bf16[2048,256]{1,0:T(8,128)(2,1)} collective-permute-done((bf16[2048,256]{1,0:T(8,128)(2,1)S(1)}, bf16[2048,256]{1,0:T(8,128)(2,1)}, u32[]{:S(2)}, u32[]{:S(2)}) %collective-permute-start.11) | collective-permute-done | bytes 1048608 | tf_op jit(solution)/shard_map/cond/branch_5_fun/ppermute | solution.py:21
  163.4 2.5 %fusion.7 = bf16[1,2048,256]{2,1,0:T(8,128)(2,1)} fusion(bf16[2048,256]{1,0:T(8,128)(2,1)} %get-tuple-element.50, bf16[2048,256]{1,0:T(8,128)(2,1)S(1)} %subtract_convert_fusion), kind=kLoop, calls=%fused_computation.11 | loop fusion | flops 2621440 | bytes 3145728 | tf_op jit(solution)/shard_map/broadcast_in_dim | solution.py:61
Async XLA Ops:
  6.5 3.3 %copy-start = (s32[2]{0:T(128)S(1)}, s32[2]{0:T(128)}, u32[]{:S(2)}) copy-start(s32[2]{0:T(128)} %param.21) | copy-start | bytes 28
  6.5 65.4 %copy-start.3 = (bf16[2,1,1024,256]{3,2,1,0:T(8,128)(2,1)S(1)}, bf16[2,1,1024,256]{3,2,1,0:T(8,128)(2,1)}, u32[]{:S(2)}) copy-start(bf16[2,1,1024,256]{3,2,1,0:T(8,128)(2,1)} %param.20) | copy-start | bytes 3145732
  6.5 65.4 %copy-start.2 = (bf16[1,2048,256]{2,1,0:T(8,128)(2,1)S(1)}, bf16[1,2048,256]{2,1,0:T(8,128)(2,1)}, u32[]{:S(2)}) copy-start(bf16[1,2048,256]{2,1,0:T(8,128)(2,1)} %param.18) | copy-start | bytes 3145732
  6.5 65.4 %copy-start.1 = (bf16[1,2048,256]{2,1,0:T(8,128)(2,1)S(1)}, bf16[1,2048,256]{2,1,0:T(8,128)(2,1)}, u32[]{:S(2)}) copy-start(bf16[1,2048,256]{2,1,0:T(8,128)(2,1)} %param.17) | copy-start | bytes 3145732
  6.5 65.4 %all-gather.5.cloned.1.call-start = ((), (), s32[]{:S(2)}) async-start(), calls=%async_computation | async-start | bytes 4718592 | tf_op jit(solution)/shard_map/all_gather | solution.py:52
  9.1 121.3 %all-gather.7.cloned.1.call-start = ((), (), s32[]{:S(2)}) async-start(), calls=%async_computation.1 | async-start | bytes 4718592 | tf_op jit(solution)/shard_map/all_gather | solution.py:52
  77.8 47.5 %collective-permute-start.1 = (bf16[2048,256]{1,0:T(8,128)(2,1)S(1)}, bf16[2048,256]{1,0:T(8,128)(2,1)}, u32[]{:S(2)}, u32[]{:S(2)}) collective-permute-start(bf16[2048,256]{1,0:T(8,128)(2,1)S(1)} %param.1), channel_id=1, source_target_pairs={{0,16},{16,0},{8,24},{24,8},{32,48},{48,32},{40,56},{56,40},{64,80... | collective-permute-start | bytes 3145736 | tf_op jit(solution)/shard_map/cond/branch_1_fun/ppermute | solution.py:21
  137.7 25.6 %collective-permute-start.11 = (bf16[2048,256]{1,0:T(8,128)(2,1)S(1)}, bf16[2048,256]{1,0:T(8,128)(2,1)}, u32[]{:S(2)}, u32[]{:S(2)}) collective-permute-start(bf16[2048,256]{1,0:T(8,128)(2,1)S(1)} %param.11), channel_id=1, source_target_pairs={{0,256},{256,0},{8,264},{264,8},{16,272},{272,16},{24,280},{280,24... | collective-permute-start | bytes 3145736 | tf_op jit(solution)/shard_map/cond/branch_5_fun/ppermute | solution.py:21
Sparse Core Ops, SparseCore 0:
  9.5 62.4 all-gather.4
  74.0 56.3 all-gather.6
where the time goes:
time: 173 us
  waiting for transfers between devices  131 us (76%)
  between operations  14.8 us (9%)
  matrix products  13.1 us (8%)
  starting transfers between devices  8.36 us (5%)
  local copies, waits for them, and re-layouts  3.12 us (2%)
  other arithmetic  2.5 us (1%)
    all_gather x2, waiting for transfers between devices, per_device(): lax.all_gather(inputs[step, 0], 'tp', axis=0, tiled=True)  65.2 us
    ppermute x2, waiting for transfers between devices, partner(): return lax.ppermute(block, axis, route)  64.9 us
    dot_general x2, matrix products, per_device(): jnp.einsum('rk,rn->kn', lax.all_gather(inputs[step, 0], 'tp', axis=0, til...  13.1 us
    ppermute x2, starting transfers between devices, partner(): return lax.ppermute(block, axis, route)  8.29 us
  transfers between devices with their start and end apart: 4, of which 4 were waited for; matrix products, arithmetic and copies ran while one was open for 4% of the time, Pallas kernels for 0%

commit v1 on v0

v1 whole, which is shorter than its diff:
```python
from functools import partial
import math

import jax
import jax.numpy as jnp
from jax import lax
from jax.experimental import pallas as pl
from jax.experimental.pallas import tpu as pltpu
from jax.sharding import PartitionSpec as P

CHUNKS = 8
FULL = 2
LAG = 2
LAST = 1
AHEAD = 4
TILE = 64
MESH = pl.DeviceIdType.MESH


def gossip_kernel(
    bit_a,
    bit_b,
    w_hbm,
    v_hbm,
    x_hbm,
    c_hbm,
    o_hbm,
    xall,
    w_own,
    v_own,
    c_own,
    c_end,
    grad,
    first,
    u0,
    u0_in,
    u1,
    u1_in,
    out,
    p_out,
    p_in,
    sem_in,
    sem_x,
    recv_n,
    recv_s,
    send_r,
    send_l,
    send_s,
    sem_a,
    sem_b,
    sem_p,
    sem_c,
    sem_o,
):
    rows = x_hbm.shape[2]
    din = x_hbm.shape[3]
    width = xall.shape[3]
    total = xall.shape[2]
    chip_rows = 2 * rows
    rest = total - chip_rows
    factor = 1.0 / math.sqrt(din)

    rep = lax.axis_index("rep")
    tp = lax.axis_index("tp")
    z = tp // 2
    core = tp % 2
    sibling = {"tp": z * 2 + 1 - core}
    right = {"tp": jnp.minimum(tp + 2, 7)}
    left = {"tp": jnp.maximum(tp - 2, 0)}
    at_a, at_b = 1 << bit_a, 1 << bit_b
    mate_a = {"rep": rep + at_a - 2 * at_a * ((rep // at_a) % 2)}
    mate_b = {"rep": rep + at_b - 2 * at_b * ((rep // at_b) % 2)}
    is_first = z == 0
    is_last = z == 3
    is_end = jnp.logical_or(is_first, is_last)
    is_mid = jnp.logical_not(is_end)
    inner = {"tp": jnp.where(is_first, 2 + core, 4 + core)}
    outer = {"tp": jnp.where(z == 1, core, 6 + core)}

    x_rows = pl.ds(pl.multiple_of(tp * rows, rows), rows)

    def load_x(s, k):
        cols = pl.ds(pl.multiple_of(k * width, width), width)
        return pltpu.make_async_copy(
            x_hbm.at[s, 0, :, cols], xall.at[s, k, x_rows, :], sem_x.at[s, k]
        )

    loads = [
        pltpu.make_async_copy(c_hbm.at[:, 0], c_own, sem_in.at[0]),
        pltpu.make_async_copy(w_hbm.at[0], w_own, sem_in.at[1]),
        pltpu.make_async_copy(v_hbm.at[0], v_own, sem_in.at[2]),
    ]

    def start_x(k, carry):
        load_x(0, k).start()
        load_x(1, k).start()
        return carry

    lax.fori_loop(0, CHUNKS, start_x, 0)
    for load in loads:
        load.start()

    barrier = pltpu.get_barrier_semaphore()
    for mate in (sibling, mate_a, mate_b):
        pl.semaphore_signal(barrier, inc=1, device_id=mate, device_id_type=MESH)

    @pl.when(z < 3)
    def _():
        pl.semaphore_signal(barrier, inc=1, device_id=right, device_id_type=MESH)

    @pl.when(z > 0)
    def _():
        pl.semaphore_signal(barrier, inc=1, device_id=left, device_id_type=MESH)

    pl.semaphore_wait(barrier, jnp.where(is_end, 4, 5))

    def block(s, k, source):
        at = pl.ds(pl.multiple_of((source * 2 + core) * rows, rows), rows)
        return xall.at[s, k, at, :]

    def hop(s, k, source, send, recv, to):
        return pltpu.make_async_remote_copy(
            src_ref=block(s, k, source),
            dst_ref=block(s, k, source),
            send_sem=send.at[source, s, k],
            recv_sem=recv.at[source, s, k],
            device_id=to,
            device_id_type=MESH,
        )

    def to_right(s, k, source):
        return hop(s, k, source, send_r, recv_n, right)

    def to_left(s, k, source):
        return hop(s, k, source, send_l, recv_n, left)

    def to_sibling(s, k, source):
        return hop(s, k, source, send_s, recv_s, sibling)

    def goes_right(k):
        return jnp.logical_or(z < 2, jnp.logical_and(z == 2, k < FULL))

    def goes_left(k):
        return jnp.logical_or(z > 1, jnp.logical_and(z == 1, k < FULL))

    def gathers(k):
        return jnp.logical_or(is_mid, k < FULL)

    def give_c(s):
        at = pl.ds(pl.multiple_of(jnp.where(is_first, chip_rows, 0), chip_rows), rest)
        return pltpu.make_async_remote_copy(
            src_ref=c_hbm.at[s, 0, at, :],
            dst_ref=c_end.at[s],
            send_sem=sem_c.at[0, s],
            recv_sem=sem_c.at[1, s],
            device_id=inner,
            device_id_type=MESH,
        )

    def give_p(s, k):
        return pltpu.make_async_remote_copy(
            src_ref=p_out.at[s, k],
            dst_ref=p_in.at[s, k],
            send_sem=sem_p.at[0, s, k],
            recv_sem=sem_p.at[1, s, k],
            device_id=outer,
            device_id_type=MESH,
        )

    def swap(k, mine, theirs, sems, mate):
        return pltpu.make_async_remote_copy(
            src_ref=mine.at[k],
            dst_ref=theirs.at[k],
            send_sem=sems.at[0, k],
            recv_sem=sems.at[1, k],
            device_id=mate,
            device_id_type=MESH,
        )

    def swap_a(k):
        return swap(k, u0, u0_in, sem_a, mate_a)

    def swap_b(k):
        return swap(k, u1, u1_in, sem_b, mate_b)

    def store(k):
        at = pl.ds(pl.multiple_of(k * width, width), width)
        return pltpu.make_async_copy(out.at[k], o_hbm.at[0, at, :], sem_o.at[k])

    def send_own(s, k):
        load_x(s, k).wait()

        @pl.when(goes_right(k))
        def _():
            to_right(s, k, z).start()

        @pl.when(goes_left(k))
        def _():
            to_left(s, k, z).start()

        to_sibling(s, k, z).start()

    def pass_on(apart, s, k):
        @pl.when(jnp.logical_and(z >= apart, gathers(k)))
        def _():
            source = z - apart
            to_right(s, k, source).wait_recv()

            @pl.when(goes_right(k))
            def _():
                to_right(s, k, source).start()

            to_sibling(s, k, source).start()

        @pl.when(jnp.logical_and(z + apart <= 3, gathers(k)))
        def _():
            source = z + apart
            to_left(s, k, source).wait_recv()

            @pl.when(goes_left(k))
            def _():
                to_left(s, k, source).start()

            to_sibling(s, k, source).start()

    def drain(s, k):
        for source in range(4):
            has = jnp.logical_or(z == source, gathers(k))

            @pl.when(jnp.logical_and(z >= source, jnp.logical_and(has, goes_right(k))))
            def _():
                to_right(s, k, source).wait_send()

            @pl.when(jnp.logical_and(z <= source, jnp.logical_and(has, goes_left(k))))
            def _():
                to_left(s, k, source).wait_send()

            @pl.when(has)
            def _():
                to_sibling(s, k, source).wait_send()

        @pl.when(jnp.logical_and(is_mid, k >= FULL))
        def _():
            give_p(s, k).wait_send()

    def product(x, c):
        return lax.dot_general(
            x, c, (((0,), (0,)), ((), ())), preferred_element_type=jnp.float32
        )

    def gradient(s, k):
        for source in range(4):

            @pl.when(jnp.logical_or(z == source, gathers(k)))
            def _():
                to_sibling(s, k, source).wait_recv()

        @pl.when(jnp.logical_and(is_mid, k >= FULL))
        def _():
            @pl.when(k == FULL)
            def _():
                give_c(s).wait_recv()

            at = pl.ds(pl.multiple_of(jnp.where(z == 1, chip_rows, 0), chip_rows), rest)
            p_out[s, k] = product(xall[s, k, at, :], c_end[s]).astype(jnp.bfloat16)
            give_p(s, k).start()

        @pl.when(gathers(k))
        def _():
            grad[...] = product(xall[s, k], c_own[s])

        @pl.when(jnp.logical_not(gathers(k)))
        def _():
            at = pl.ds(pl.multiple_of(z * chip_rows, chip_rows), chip_rows)
            grad[...] = product(xall[s, k, at, :], c_own[s, at, :])
            give_p(s, k).wait_recv()
            grad[...] += p_in[s, k].astype(jnp.float32)

    def tiles(body):
        def run(t, carry):
            body(pl.ds(pl.multiple_of(t * TILE, TILE), TILE), t * TILE)
            return carry

        lax.fori_loop(0, width // TILE, run, 0)

    def first_step(k):
        gradient(0, k)

        @pl.when(k == 0)
        def _():
            loads[1].wait()
            loads[2].wait()

        def body(at, low):
            whole = pl.ds(pl.multiple_of(k * width + low, TILE), TILE)
            g = grad[at, :] * factor
            m = 0.1 * g
            v = 0.95 * v_own[whole, :].astype(jnp.float32) + 0.05 * g * g
            u = w_own[whole, :].astype(jnp.float32) - 0.2 * m / (jnp.sqrt(v) + 1e-08)
            u0[k, at, :] = u.astype(jnp.bfloat16)
            first[whole, :] = m.astype(jnp.bfloat16)
            v_own[whole, :] = v.astype(jnp.bfloat16)

        tiles(body)
        swap_a(k).start()

    def second_step(k):
        gradient(1, k)
        swap_a(k).wait_recv()

        def body(at, low):
            whole = pl.ds(pl.multiple_of(k * width + low, TILE), TILE)
            g = grad[at, :] * factor
            m = 0.9 * first[whole, :].astype(jnp.float32) + 0.1 * g
            v = 0.95 * v_own[whole, :].astype(jnp.float32) + 0.05 * g * g
            w = (u0[k, at, :].astype(jnp.float32) + u0_in[k, at, :].astype(jnp.float32)) * 0.5
            w = w.astype(jnp.bfloat16).astype(jnp.float32)
            u = w - 0.2 * m / (jnp.sqrt(v) + 1e-08)
            u1[k, at, :] = u.astype(jnp.bfloat16)

        tiles(body)
        swap_b(k).start()

    def finish(k):
        swap_b(k).wait_recv()

        def body(at, low):
            w = (u1[k, at, :].astype(jnp.float32) + u1_in[k, at, :].astype(jnp.float32)) * 0.5
            out[k, at, :] = w.astype(jnp.bfloat16)

        tiles(body)
        store(k).start()

    def each(i, act):
        @pl.when(jnp.logical_and(i >= 0, i < CHUNKS))
        def _():
            act(0, i)

        @pl.when(jnp.logical_and(i >= LAG, i < CHUNKS + LAG))
        def _():
            act(1, i - LAG)

    def turn(i, carry):
        each(i + AHEAD, send_own)

        if FULL < CHUNKS:

            @pl.when(jnp.logical_and(i == -1, is_end))
            def _():
                give_c(0).start()
                give_c(1).start()

        each(i + 2, partial(pass_on, 1))
        each(i + 1, partial(pass_on, 2))
        each(i, partial(pass_on, 3))

        @pl.when(i == 0)
        def _():
            loads[0].wait()

        @pl.when(jnp.logical_and(i >= 0, i < CHUNKS))
        def _():
            first_step(i)

        @pl.when(jnp.logical_and(i >= LAG, i < CHUNKS + LAG))
        def _():
            second_step(i - LAG)

        @pl.when(i >= LAG + LAST)
        def _():
            finish(i - LAG - LAST)

        each(i - 1, drain)
        return carry

    lax.fori_loop(-AHEAD, CHUNKS + LAG + LAST, turn, 0)

    if FULL < CHUNKS:

        @pl.when(is_end)
        def _():
            give_c(0).wait_send()
            give_c(1).wait_send()

    def finish_sends(k, carry):
        swap_a(k).wait_send()
        swap_b(k).wait_send()
        store(k).wait()
        return carry

    lax.fori_loop(0, CHUNKS, finish_sends, 0)


def run_pair(number, bit_a, bit_b, weight, second, inputs, cotangent):
    _, din, cols = weight.shape
    steps, _, rows, _ = inputs.shape
    total = cotangent.shape[2]
    width = din // CHUNKS
    half = jnp.bfloat16
    piece = (CHUNKS, width, cols)
    dma = pltpu.SemaphoreType.DMA
    return pl.pallas_call(
        partial(gossip_kernel, bit_a, bit_b),
        out_shape=jax.ShapeDtypeStruct(weight.shape, weight.dtype),
        in_specs=[pl.BlockSpec(memory_space=pl.ANY)] * 4,
        out_specs=pl.BlockSpec(memory_space=pl.ANY),
        scratch_shapes=[
            pltpu.VMEM((steps, CHUNKS, total, width), half),
            pltpu.VMEM((din, cols), half),
            pltpu.VMEM((din, cols), half),
            pltpu.VMEM((steps, total, cols), half),
            pltpu.VMEM((steps, total - 2 * rows, cols), half),
            pltpu.VMEM((width, cols), jnp.float32),
            pltpu.VMEM((din, cols), half),
            pltpu.VMEM(piece, half),
            pltpu.VMEM(piece, half),
            pltpu.VMEM(piece, half),
            pltpu.VMEM(piece, half),
            pltpu.VMEM(piece, half),
            pltpu.VMEM((steps,) + piece, half),
            pltpu.VMEM((steps,) + piece, half),
            dma((3,)),
            dma((steps, CHUNKS)),
            dma((4, steps, CHUNKS)),
            dma((4, steps, CHUNKS)),
            dma((4, steps, CHUNKS)),
            dma((4, steps, CHUNKS)),
            dma((4, steps, CHUNKS)),
            dma((2, CHUNKS)),
            dma((2, CHUNKS)),
            dma((2, steps, CHUNKS)),
            dma((2, steps)),
            dma((CHUNKS,)),
        ],
        compiler_params=pltpu.CompilerParams(
            collective_id=number, has_side_effects=True, vmem_limit_bytes=48 << 20
        ),
    )(weight, second, inputs, cotangent)


def per_device(weight, second_moment, inputs, cotangent, gossip_steps):
    top = lax.axis_size("rep").bit_length() - 2
    pairs = [(top, low) for low in range(top)] + [(low, top) for low in range(top)]
    branches = [partial(run_pair, n, a, b) for n, (a, b) in enumerate(pairs)]
    which = jnp.where(gossip_steps[0] == top, gossip_steps[1], top + gossip_steps[0])
    return lax.switch(which, branches, weight, second_moment, inputs, cotangent)


def solution(mesh):
    in_specs = (
        P("rep", None, "tp"),
        P("rep", None, "tp"),
        P(None, "rep", "tp", None),
        P(None, "rep", None, "tp"),
        P(),
    )
    out_specs = P("rep", None, "tp")
    return jax.shard_map(
        per_device, mesh=mesh, in_specs=in_specs, out_specs=out_specs, check_vma=False
    )
```

time: 173 us -> 108 us (0.62)
  the two profiles are of different devices: /device:TPU:2 before, /device:TPU:50 now
where the time goes in v1:
time: 108 us
  Pallas kernels  103 us (95%)
  local copies, waits for them, and re-layouts  2.21 us (2%)
  between operations  1.88 us (2%)
    pallas_call x1, Pallas kernels, run_pair(): pl.pallas_call(partial(gossip_kernel, bit_a, bit_b), out_shape=jax.ShapeD...  103 us

profile of v1, /device:TPU:50, one launch (start us, length us, event | category | flops | bytes accessed | tf_op | source)
XLA Modules:
  0.0 107.8 jit_solution(17656299199645858646)
XLA Ops:
  0.0 0.0 copy-start
  0.0 0.7 copy-done
  0.7 0.6 fusion
  3.1 103.7 %conditional.1 = (bf16[1,2048,256]{2,1,0:T(8,128)(2,1)S(1)}) conditional(s32[]{:T(128)} %bitcast, (bf16[1,2048,256]{2,1,0:T(8,128)(2,1)}, bf16[1,2048,256]{2,1,0:T(8,128)(2,1)}, bf16[2,1,128,2048]{3,2,1,0:T(8,128)(2,1)}, bf16[2,1,1024,256]{3,2,1,0:T(8,128)(2,1)}) %tuple.35, (bf16[1,2048,256]{2,1,0:T(8,128)(2,1)}, ...), branch_computations={%region_0.1_spmd, %region_1.2_spmd, %region_2.3_spmd, %region_3.4_... | conditional | bytes 8 | solution.py:446
  3.1 103.1 %branch_2_fun.1 = bf16[1,2048,256]{2,1,0:T(8,128)(2,1)S(1)} custom-call(bf16[1,2048,256]{2,1,0:T(8,128)(2,1)} %get-tuple-element.104.w_hbm, bf16[1,2048,256]{2,1,0:T(8,128)(2,1)} %get-tuple-element.105.v_hbm, bf16[2,1,128,2048]{3,2,1,0:T(8,128)(2,1)} %get-tuple-element.106.x_hbm, bf16[2,1,1024,256]{3,2,1,0:T(8,128)(2,1)} %get-tuple-element.107.c_hbm), custom_call_target="tpu_custom_call" | custom-call | tf_op jit(solution)/shard_map/cond/branch_2_fun/pallas_call | solution.py:402
  106.8 1.0 copy.27
Async XLA Ops:
  0.0 0.7 copy-start
